TPU v7x, 32 devices: a whole 2x2x4 slice. The times are simulated.
32 devices in a mesh: ctx: 8 (over z, y), tp: 4 (over x, core).
Axes of the slice: x: 2, y: 2, z: 4, core: 2. Of those that a mesh axis runs over, the one named last changes fastest.
Arguments:
- features: bfloat16 [1024, 3, 4096], P('ctx', None, 'tp'), may hold values from -6 to 6
- short_taps: float32 [3, 3, 4096], P(None, None, 'tp'), may hold values from -3 to 3
- residues: float32 [16, 4096], P(None, 'tp'), may hold values from -2 to 2
- log_rate: float32 [16, 4096], P(None, 'tp'), may hold values from -13 to -3.5, as said below
- out_weight: bfloat16 [4096, 8192], P('tp'), may hold values from -0.09375 to 0.09375
- grad_out: bfloat16 [1024, 8192], P('ctx', 'tp'), may hold values from -6 to 6
Outputs:
- grad_features: bfloat16 [1024, 3, 4096], P('ctx', None, 'tp')
- grad_taps: float32 [3, 3, 4096], P(None, None, 'tp')
- grad_residues: float32 [16, 4096], P(None, 'tp')
- grad_log_rate: float32 [16, 4096], P(None, 'tp')
- grad_weight_t: float32 [8192, 4096], P('ctx', 'tp')
Inputs may be any that keep to these rules, and one draw needn't show every extreme that they name: `log_rate`: log of a decay rate per token.
All inputs are finite; a program needn't handle non-finite values.
Results may differ from a plain program's by a relative error of at most 0.0058.
Values may be sent and summed in bfloat16 or wider, within the bound.
A program may use at most 192 MiB of HBM per device.

v0:
```python
import jax
import jax.numpy as jnp
from jax import lax
from jax.sharding import PartitionSpec as P


def shifted(value, axis, steps):
    count = lax.axis_size(axis)
    first, last = (max(0, -steps), min(count, count - steps))
    return lax.ppermute(value, axis, [(source, source + steps) for source in range(first, last)])


def block_tables(residues, log_rate, block_len):
    decay_rate = jnp.exp(log_rate)
    amplitude = residues * jnp.exp(0.5 * log_rate)
    lag_steps = jnp.arange(block_len).astype(jnp.float32)
    kernel = jnp.sum(
        amplitude[:, None, :] * jnp.exp(-decay_rate[:, None, :] * lag_steps[None, :, None]), axis=0
    )
    row_ids = jnp.arange(block_len)[:, None]
    col_ids = jnp.arange(block_len)[None, :]
    distance = row_ids - col_ids
    toeplitz = jnp.where((distance >= 0)[:, :, None], kernel[jnp.maximum(distance, 0)], 0.0)
    injection = jnp.exp(-decay_rate[:, None, :] * (block_len - 1 - lag_steps)[None, :, None])
    readout = amplitude[:, None, :] * jnp.exp(
        -decay_rate[:, None, :] * (lag_steps + 1.0)[None, :, None]
    )
    return (decay_rate, toeplitz, injection, readout)


def combine_states(earlier, later):
    return (earlier[0] * later[0], later[0] * earlier[1] + later[1])


def long_conv(product, residues, log_rate):
    block_len = 128
    length, channels = product.shape
    block_count = length // block_len
    decay_rate, toeplitz, injection, readout = block_tables(residues, log_rate, block_len)
    blocks = product.reshape(block_count, block_len, channels)
    inside = jnp.einsum("ijc,bjc->bic", toeplitz, blocks, precision=lax.Precision.HIGHEST)
    entering = jnp.einsum("rjc,bjc->brc", injection, blocks, precision=lax.Precision.HIGHEST)
    carry_decay = jnp.broadcast_to(jnp.exp(-decay_rate * block_len), entering.shape)
    unused, states = lax.associative_scan(combine_states, (carry_decay, entering), axis=0)
    before = jnp.concatenate([jnp.zeros_like(states[:1]), states[:-1]], axis=0)
    from_past = jnp.einsum("ric,brc->bic", readout, before, precision=lax.Precision.HIGHEST)
    return (inside + from_past).reshape(length, channels)


def to_channels(values):
    return lax.all_to_all(values, "ctx", split_axis=1, concat_axis=0, tiled=True)


def to_tokens(values):
    return lax.all_to_all(values, "ctx", split_axis=0, concat_axis=1, tiled=True)


def per_device(features, short_taps, residues, log_rate, out_weight, grad_out):
    length = features.shape[0]
    tap_count = short_taps.shape[0]
    groups = lax.axis_size("ctx")
    position = lax.axis_index("ctx")
    rim_rows = shifted(features[length - (tap_count - 1) :], "ctx", 1)
    padded_in = jnp.concatenate([rim_rows, features], axis=0).astype(jnp.float32)
    shortened = sum(
        (
            short_taps[lag] * padded_in[tap_count - 1 - lag : tap_count - 1 - lag + length]
            for lag in range(tap_count)
        )
    )
    product = (shortened[:, 1] * shortened[:, 2]).astype(jnp.bfloat16)
    chan_width = product.shape[1] // groups
    local_residues = lax.dynamic_slice_in_dim(residues, position * chan_width, chan_width, 1)
    local_rates = lax.dynamic_slice_in_dim(log_rate, position * chan_width, chan_width, 1)
    product_chan = to_channels(product).astype(jnp.float32)
    conv_chan, pullback = jax.vjp(long_conv, product_chan, local_residues, local_rates)
    convolved = to_tokens(conv_chan.astype(jnp.bfloat16)).astype(jnp.float32)
    gated = (shortened[:, 0] * convolved).astype(jnp.bfloat16)
    cotangent = lax.all_gather(grad_out, "tp", axis=1, tiled=True)
    grad_weight_t = lax.psum_scatter(
        lax.dot_general(
            cotangent, gated, (((0,), (0,)), ((), ())), preferred_element_type=jnp.float32
        ),
        "ctx",
        scatter_dimension=0,
        tiled=True,
    )
    grad_gated = lax.dot_general(
        cotangent, out_weight, (((1,), (1,)), ((), ())), preferred_element_type=jnp.float32
    )
    grad_conv = (grad_gated * shortened[:, 0]).astype(jnp.bfloat16)
    grad_prod_chan, grad_res_local, grad_rate_local = pullback(
        to_channels(grad_conv).astype(jnp.float32)
    )
    grad_product = to_tokens(grad_prod_chan.astype(jnp.bfloat16)).astype(jnp.float32)
    grad_residues, grad_log_rate = (
        lax.all_gather(grad_res_local, "ctx", axis=1, tiled=True),
        lax.all_gather(grad_rate_local, "ctx", axis=1, tiled=True),
    )
    grad_short = jnp.stack(
        [grad_gated * convolved, grad_product * shortened[:, 2], grad_product * shortened[:, 1]],
        axis=1,
    )
    tail_rows = shifted(grad_short[: tap_count - 1], "ctx", -1)
    tail_pad = jnp.concatenate([grad_short, tail_rows], axis=0)
    grad_features = sum(
        (short_taps[lag] * tail_pad[lag : lag + length] for lag in range(tap_count))
    )
    partial_taps = jnp.stack(
        [
            jnp.sum(
                grad_short * padded_in[tap_count - 1 - lag : tap_count - 1 - lag + length], axis=0
            )
            for lag in range(tap_count)
        ],
        axis=0,
    )
    grad_taps = lax.psum(partial_taps, "ctx")
    return (
        grad_features.astype(jnp.bfloat16),
        grad_taps,
        grad_residues,
        grad_log_rate,
        grad_weight_t,
    )


def solution(mesh):
    return jax.shard_map(
        per_device,
        mesh=mesh,
        in_specs=(
            P("ctx", None, "tp"),
            P(None, None, "tp"),
            P(None, "tp"),
            P(None, "tp"),
            P("tp", None),
            P("ctx", "tp"),
        ),
        out_specs=(
            P("ctx", None, "tp"),
            P(None, None, "tp"),
            P(None, "tp"),
            P(None, "tp"),
            P("ctx", "tp"),
        ),
        check_vma=False,
    )
```

profile of v0, /device:TPU:0, one launch (start us, length us, event | category | flops | bytes accessed | tf_op | source)
XLA Modules:
  0.0 879.5 jit_solution(6375209423134570061)
XLA Ops:
  8.7 4.9 collective-permute-start
  16.3 1.4 maximum_convert_fusion
  18.9 1.8 copy.151
  20.7 5.3 all-to-all-start
  28.0 6.5 all-to-all-done
  34.5 2.8 fusion.16
  37.4 1.2 copy.128
  38.6 13.0 %multiply_convert_fusion.1 = (bf16[128,1024]{1,0:T(8,128)(2,1)}, f32[128,1024]{1,0:T(8,128)}) fusion(f32[128,3,1024]{2,0,1:T(8,128)S(1)} %multiply_add_fusion, bf16[128,8192]{1,0:T(8,128)(2,1)} %all-gather.2.cloned.1.call-done, bf16[1024,8192]{1,0:T(8,128)(2,1)} %param.10), kind=kOutput, calls=%fused_computation.43 | convolution fusion | flops 2147745792 | bytes 20185088 | tf_op jit(solution)/shard_map/dot_general | solution.py:88
  51.6 1.8 copy.153
  53.4 4.1 all-to-all-start.2
  60.4 3.2 pad.240
  63.6 2.0 all-to-all-done.2
  65.7 3.0 fusion.11
  68.7 1.8 copy.134
  72.0 1.3 pad_maximum_fusion.3
  73.3 1.8 pad.157
  76.0 1.0 copy.156
  77.0 3.3 fusion.13
  80.3 5.6 select_bitcast_fusion
  85.9 9.3 %copy.155 = f32[128,128,128]{2,1,0:T(8,128)} copy(f32[128,128,128]{1,0,2:T(8,128)} %select_bitcast_fusion) | data formatting | bytes 16777216 | tf_op jit(solution)/shard_map/transpose(jvp(jit(_where)))/select_n | solution.py:23
  95.2 98.8 %scatter_custom_fusion = f32[128,128]{1,0:T(8,128)S(1)} fusion(s32[16384]{0:T(1024)} %maximum_bitcast_fusion, f32[16384,128]{1,0:T(8,128)} %bitcast.83, f32[]{:T(128)} %constant.7.clone.1), kind=kCustom, calls=%fused_computation.85 | custom fusion | flops 2097152 | bytes 66048 | tf_op jit(solution)/shard_map/transpose(jvp())/scatter-add | solution.py:23
  194.8 4.6 multiply_reduce_fusion.4
  200.3 54.8 %gather_fusion = f32[16384,128]{1,0:T(8,128)} fusion(f32[128,128]{1,0:T(8,128)S(1)} %copy.124, s32[16384]{0:T(1024)S(1)} %broadcast_clamp_fusion), kind=kCustom, calls=%fused_computation | custom fusion | bytes 16842752 | tf_op jit(solution)/shard_map/jvp()/gather | solution.py:23
  255.1 9.9 %broadcast_select_fusion = f32[128,128,128]{2,1,0:T(8,128)} fusion(f32[128,128,128]{2,1,0:T(8,128)} %bitcast.82, pred[128,128]{1,0:T(8,128)(4,1)} %subtract_compare_fusion), kind=kLoop, calls=%fused_computation.4 | loop fusion | flops 2097152 | bytes 16793600 | tf_op jit(solution)/shard_map/jvp(jit(_where))/select_n | solution.py:23
  265.1 9.3 %copy.126 = f32[128,128,128]{1,0,2:T(8,128)} copy(f32[128,128,128]{2,1,0:T(8,128)} %broadcast_select_fusion) | data formatting | bytes 16777216 | tf_op jit(solution)/shard_map/jvp(jit(_where))/select_n | solution.py:23
  274.3 10.1 %fusion.9 = bf16[8,128,128]{1,0,2:T(8,128)(2,1)S(1)} fusion(f32[128,8,128]{2,1,0:T(8,128)} %fusion.13, f32[128,128,128]{1,0,2:T(8,128)} %copy.126, bf16[128,8,128]{0,2,1:T(8,128)(2,1)} %all-to-all-done), kind=kOutput, calls=%fused_computation.26 | convolution fusion | flops 201588736 | bytes 9437184 | tf_op jit(solution)/shard_map/jvp(ijc,bjc->bic)/dot_general | solution.py:41
  284.5 12.0 %all_to_all.43 = bf16[8,128,128]{1,2,0:T(8,128)(2,1)S(1)} all-to-all(bf16[8,128,128]{1,2,0:T(8,128)(2,1)S(1)} %copy.130), channel_id=1, replica_groups=mesh['ctx'=8,'tp'=4] {'ctx'}, dimensions={0} | all-to-all | bytes 524288 | tf_op jit(solution)/shard_map/all_to_all | solution.py:55
  297.3 2.0 copy.152
  299.4 17.4 %convolution_bitcast_fusion = f32[8192,1024]{0,1:T(8,128)} fusion(bf16[128,8192]{1,0:T(8,128)(2,1)} %all-gather.2.cloned.1.call-done, f32[128,1024]{1,0:T(8,128)} %copy.152, f32[128,3,1024]{2,0,1:T(8,128)S(1)} %multiply_add_fusion), kind=kOutput, calls=%fused_computation.2 | convolution fusion | flops 2147745792 | bytes 36700160 | tf_op jit(solution)/shard_map/dot_general | solution.py:81
  316.8 1.3 split.21
  320.3 1.9 pad.134
  322.2 1.4 multiply_add_fusion.1
  323.8 2.6 pad.113
  327.3 1.0 copy.135
  328.3 2.2 fusion.15
  330.5 7.5 fusion.8
  338.7 4.1 all-to-all-start.3
  342.8 3.3 fusion.5
  351.6 32.6 %all_gather.11 = f32[16,1024]{1,0:T(8,128)S(1)} all-gather(f32[16,128]{1,0:T(8,128)S(1)} %get-tuple-element.56), channel_id=1, replica_groups=mesh['ctx'=8,'tp'=4] {'ctx'}, dimensions={1}, use_global_device_ids=true | all-gather | bytes 73728 | tf_op jit(solution)/shard_map/all_gather | solution.py:98
  384.2 1.8 convert_element_type.104
  386.0 2.0 copy.154
  388.0 1.3 multiply_bitcast_fusion
  389.6 1.3 collective-permute-start.1
  391.0 32.0 %all_gather.10 = f32[16,1024]{1,0:T(8,128)S(1)} all-gather(f32[16,128]{1,0:T(8,128)S(1)} %get-tuple-element.57), channel_id=1, replica_groups=mesh['ctx'=8,'tp'=4] {'ctx'}, dimensions={1}, use_global_device_ids=true | all-gather | bytes 73728 | tf_op jit(solution)/shard_map/all_gather | solution.py:97
  423.2 1.9 multiply_reduce_fusion.2
  425.1 40.6 %psum.7 = f32[3,3,1024]{2,1,0:T(4,128)} all-reduce(f32[3,3,1024]{2,1,0:T(4,128)S(1)} %pad_maximum_fusion.2), channel_id=1, replica_groups=mesh['ctx'=8,'tp'=4] {'ctx'}, use_global_device_ids=true, to_apply=%region_4.5 | all-reduce | flops 9216 | bytes 73728 | tf_op jit(solution)/shard_map/psum | solution.py:118
  465.8 400.1 %reduce-scatter.2.cloned.1.call-done = f32[1024,1024]{0,1:T(8,128)} async-done(((f32[8192,1024]{0,1:T(8,128)}), f32[1024,1024]{0,1:T(8,128)}) %reduce-scatter.2.cloned.1.call-update) | async-done | bytes 4194320 | tf_op jit(solution)/shard_map/reduce_scatter | solution.py:80
  865.8 5.3 copy.150
  (119 shorter events, 26.1 us)
Async XLA Ops:
  7.2 31.5 %all-gather.2.cloned.1.call-start = ((), (), s32[]{:S(2)}) async-start(), calls=%async_computation.5 | async-start | bytes 2621440 | tf_op jit(solution)/shard_map/all_gather | solution.py:79
  8.7 7.6 collective-permute-start
  13.6 20.9 %copy-start.20 = (f32[128]{0:T(128)}, f32[128]{0:T(128)S(1)}, u32[]{:S(2)}) copy-start(f32[128]{0:T(128)S(1)} %broadcast_subtract_fusion) | copy-start | bytes 1540
  15.0 23.6 %copy-start.15 = (f32[16,128]{1,0:T(8,128)}, f32[16,128]{1,0:T(8,128)S(1)}, u32[]{:S(2)}) copy-start(f32[16,128]{1,0:T(8,128)S(1)} %get-tuple-element.51) | copy-start | bytes 24580
  15.8 2.4 copy-start.3
  15.8 2.4 copy-start.5
  15.8 2.4 copy-start.7
  20.7 13.8 %all-to-all-start = ((bf16[128,8,128]{0,2,1:T(8,128)(2,1)}), bf16[128,8,128]{0,2,1:T(8,128)(2,1)}, u32[]{:S(2)}, u32[]{:S(2)}) async-start(bf16[128,8,128]{0,2,1:T(8,128)(2,1)} %bitcast.87), calls=%async_computation | async-start | bytes 524288 | tf_op jit(solution)/shard_map/all_to_all | solution.py:51
  38.6 19.2 %copy-start.17 = (f32[2,16,128]{2,1,0:T(8,128)}, f32[2,16,128]{2,1,0:T(8,128)S(1)}, u32[]{:S(2)}) copy-start(f32[2,16,128]{2,1,0:T(8,128)S(1)} %slice_add_fusion.3) | copy-start | bytes 49156
  53.4 12.3 %all-to-all-start.2 = ((bf16[128,8,128]{0,2,1:T(8,128)(2,1)}), bf16[128,8,128]{0,2,1:T(8,128)(2,1)}, u32[]{:S(2)}, u32[]{:S(2)}) async-start(bf16[128,8,128]{0,2,1:T(8,128)(2,1)} %bitcast.86), calls=%async_computation.2 | async-start | bytes 524288 | tf_op jit(solution)/shard_map/all_to_all | solution.py:51
  57.5 808.4 %reduce-scatter.2.cloned.1.call-start = ((), (), s32[]{:S(2)}) async-start(), calls=%async_computation.6 | async-start | bytes 37748736 | tf_op jit(solution)/shard_map/reduce_scatter | solution.py:80
  57.8 0.6 copy-start.11
  57.8 0.6 copy-start.13
  71.4 2.0 copy-start.10
  77.0 3.3 copy-start.2
  316.8 1.4 copy-start.1
  316.8 1.4 copy-start.12
  316.8 1.4 copy-start.14
  316.8 2.0 copy-start.18
  316.8 2.0 copy-start.16
  316.8 2.0 copy-start.22
  330.5 12.3 %copy-start.21 = (f32[128]{0:T(128)S(1)}, f32[128]{0:T(128)}, u32[]{:S(2)}) copy-start(f32[128]{0:T(128)} %copy-done.20) | copy-start | bytes 1540
  338.0 8.2 copy-start.19
  338.0 8.2 copy-start.9
  338.7 45.5 %all-to-all-start.3 = ((bf16[8,128,128]{1,2,0:T(8,128)(2,1)}), bf16[8,128,128]{1,2,0:T(8,128)(2,1)}, u32[]{:S(2)}, u32[]{:S(2)}) async-start(bf16[8,128,128]{1,2,0:T(8,128)(2,1)} %copy.137), calls=%async_computation.3 | async-start | bytes 524288 | tf_op jit(solution)/shard_map/all_to_all | solution.py:55
  388.0 1.4 copy-start
  389.6 33.3 %collective-permute-start.1 = (f32[2,3,1024]{2,0,1:T(2,128)S(1)}, f32[2,3,1024]{2,0,1:T(2,128)S(1)}, u32[]{:S(2)}, u32[]{:S(2)}) collective-permute-start(f32[2,3,1024]{2,0,1:T(2,128)S(1)} %slice.179), channel_id=1, source_target_pairs={{4,0},{8,4},{12,8},{16,12},{20,16},{24,20},{28,24},{5,1},{9,5},{13... | collective-permute-start | bytes 73736 | tf_op jit(solution)/shard_map/ppermute | solution.py:10
  390.9 32.3 %copy-start.4 = (f32[3,1024]{1,0:T(4,128)S(1)}, f32[3,1024]{1,0:T(4,128)}, u32[]{:S(2)}) copy-start(f32[3,1024]{1,0:T(4,128)} %copy-done.3) | copy-start | bytes 36868
  390.9 32.3 %copy-start.6 = (f32[3,1024]{1,0:T(4,128)S(1)}, f32[3,1024]{1,0:T(4,128)}, u32[]{:S(2)}) copy-start(f32[3,1024]{1,0:T(4,128)} %copy-done.5) | copy-start | bytes 36868
  390.9 32.3 %copy-start.8 = (f32[3,1024]{1,0:T(4,128)S(1)}, f32[3,1024]{1,0:T(4,128)}, u32[]{:S(2)}) copy-start(f32[3,1024]{1,0:T(4,128)} %copy-done.7) | copy-start | bytes 36868
Sparse Core Ops, SparseCore 0:
  9.6 25.2 all-gather.1
  317.0 548.8 reduce-scatter.1
where the time goes:
time: 888 us; the launch traced here: 879 us
  waiting for transfers between devices  409 us (46%)
  other arithmetic  129 us (15%)
  blocking collectives  117 us (13%)
  local copies, waits for them, and re-layouts  116 us (13%)
  matrix products  72.8 us (8%)
  starting transfers between devices  20 us (2%)
  between operations  14.8 us (2%)
    reduce_scatter x1, waiting for transfers between devices, per_device(): lax.psum_scatter(lax.dot_general(cotangent, gated, (((0,), (0,)), ((), ()...  400 us
    scatter-add x1, other arithmetic, block_tables(): kernel[jnp.maximum(distance, 0)]  98.8 us
    gather x1, local copies, waits for them, and re-layouts, block_tables(): kernel[jnp.maximum(distance, 0)]  54.8 us
    psum x1, blocking collectives, per_device(): grad_taps = lax.psum(partial_taps, 'ctx')  40.6 us
    all_gather x1, blocking collectives, per_device(): lax.all_gather(grad_rate_local, 'ctx', axis=1, tiled=True)  32.6 us
    all_gather x1, blocking collectives, per_device(): lax.all_gather(grad_res_local, 'ctx', axis=1, tiled=True)  32 us
    dot_general x3, matrix products, long_conv(): jnp.einsum('ijc,bjc->bic', toeplitz, blocks, precision=lax.Precision.HIGH...  23.2 us
    select_n x2, local copies, waits for them, and re-layouts, block_tables(): jnp.where((distance >= 0)[:, :, None], kernel[jnp.maximum(distance, 0)],...  18.6 us
  transfers between devices with their start and end apart: 7, of which 3 were waited for; matrix products, arithmetic and copies ran while one was open for 7% of the time, Pallas kernels for 0%

commit v1 on v0

--- a/solution.py
+++ b/solution.py
@@ -115,7 +115,13 @@
         ],
         axis=0,
     )
-    grad_taps = lax.psum(partial_taps, "ctx")
+    count_2 = lax.axis_size("ctx")
+    grad_taps, stride = (partial_taps, 1)
+    while stride < count_2:
+        grad_taps = grad_taps + lax.ppermute(
+            grad_taps, "ctx", [(i, i ^ stride) for i in range(count_2)]
+        )
+        stride = 2 * stride
     return (
         grad_features.astype(jnp.bfloat16),
         grad_taps,

time: 888 us -> 888 us (level)
  waiting for transfers between devices: 409 us -> 434 us
  blocking collectives: 117 us -> 94.6 us
    psum x1 -> x0, blocking collectives: 40.6 us -> none  [per_device(): grad_taps = lax.psum(partial_taps, 'ctx')]
    all_to_all x1 -> x2, blocking collectives: 12 us -> 31.2 us  [to_tokens(): lax.all_to_all(values, 'ctx', split_axis=0, concat_axis=1, tiled=True)]
    reduce_scatter x1, waiting for transfers between devices: 400 us -> 418 us  [per_device(): lax.psum_scatter(lax.dot_general(cotangent, gated, (((0,), (0,)), ((), ()...]
  transfers between devices with their start and end apart: 7 -> 9, of which waited for: 3 -> 5; matrix products, arithmetic and copies ran while one was open for 7% -> 6% of each run, Pallas kernels for 0% -> 0%
where the time goes in v1:
time: 888 us; the launch traced here: 881 us
  waiting for transfers between devices  434 us (49%)
  other arithmetic  130 us (15%)
  local copies, waits for them, and re-layouts  115 us (13%)
  blocking collectives  94.6 us (11%)
  matrix products  72.6 us (8%)
  starting transfers between devices  19.3 us (2%)
  between operations  14.9 us (2%)
    reduce_scatter x1, waiting for transfers between devices, per_device(): lax.psum_scatter(lax.dot_general(cotangent, gated, (((0,), (0,)), ((), ()...  418 us
    scatter-add x1, other arithmetic, block_tables(): kernel[jnp.maximum(distance, 0)]  98.8 us
    gather x1, local copies, waits for them, and re-layouts, block_tables(): kernel[jnp.maximum(distance, 0)]  54.8 us
    all_gather x1, blocking collectives, per_device(): lax.all_gather(grad_rate_local, 'ctx', axis=1, tiled=True)  31.8 us
    all_gather x1, blocking collectives, per_device(): lax.all_gather(grad_res_local, 'ctx', axis=1, tiled=True)  31.6 us
    all_to_all x2, blocking collectives, to_tokens(): lax.all_to_all(values, 'ctx', split_axis=0, concat_axis=1, tiled=True)  31.2 us
    dot_general x3, matrix products, long_conv(): jnp.einsum('ijc,bjc->bic', toeplitz, blocks, precision=lax.Precision.HIGH...  23.2 us
    select_n x2, local copies, waits for them, and re-layouts, block_tables(): jnp.where((distance >= 0)[:, :, None], kernel[jnp.maximum(distance, 0)],...  18.7 us
  transfers between devices with their start and end apart: 9, of which 5 were waited for; matrix products, arithmetic and copies ran while one was open for 6% of the time, Pallas kernels for 0%

profile of v1, /device:TPU:0, one launch (start us, length us, event | category | flops | bytes accessed | tf_op | source)
XLA Modules:
  0.0 880.6 jit_solution(10229562988520164522)
XLA Ops:
  8.7 4.9 collective-permute-start
  16.4 1.4 maximum_convert_fusion
  19.0 1.8 copy.151
  20.8 5.2 all-to-all-start
  28.1 6.5 all-to-all-done
  34.6 2.8 fusion.16
  37.5 1.2 copy.128
  38.7 13.0 %multiply_convert_fusion.1 = (bf16[128,1024]{1,0:T(8,128)(2,1)}, f32[128,1024]{1,0:T(8,128)}) fusion(f32[128,3,1024]{2,0,1:T(8,128)S(1)} %multiply_add_fusion, bf16[128,8192]{1,0:T(8,128)(2,1)} %all-gather.2.cloned.1.call-done, bf16[1024,8192]{1,0:T(8,128)(2,1)} %param.10), kind=kOutput, calls=%fused_computation.43 | convolution fusion | flops 2147745792 | bytes 20185088 | tf_op jit(solution)/shard_map/dot_general | solution.py:88
  51.7 1.8 copy.153
  53.5 4.1 all-to-all-start.2
  60.5 3.2 pad.246
  63.7 2.0 all-to-all-done.2
  65.8 3.0 fusion.11
  68.8 1.8 copy.134
  72.1 1.3 pad_maximum_fusion.3
  73.5 1.8 pad.157
  77.1 3.3 fusion.13
  80.4 5.6 select_bitcast_fusion
  86.0 9.4 %copy.155 = f32[128,128,128]{2,1,0:T(8,128)} copy(f32[128,128,128]{1,0,2:T(8,128)} %select_bitcast_fusion) | data formatting | bytes 16777216 | tf_op jit(solution)/shard_map/transpose(jvp(jit(_where)))/select_n | solution.py:23
  95.4 98.8 %scatter_custom_fusion = f32[128,128]{1,0:T(8,128)S(1)} fusion(s32[16384]{0:T(1024)} %maximum_bitcast_fusion, f32[16384,128]{1,0:T(8,128)} %bitcast.83, f32[]{:T(128)} %constant.7.clone.1), kind=kCustom, calls=%fused_computation.85 | custom fusion | flops 2097152 | bytes 66048 | tf_op jit(solution)/shard_map/transpose(jvp())/scatter-add | solution.py:23
  194.9 4.6 multiply_reduce_fusion.4
  200.5 54.8 %gather_fusion = f32[16384,128]{1,0:T(8,128)} fusion(f32[128,128]{1,0:T(8,128)S(1)} %copy.124, s32[16384]{0:T(1024)S(1)} %broadcast_clamp_fusion), kind=kCustom, calls=%fused_computation | custom fusion | bytes 16842752 | tf_op jit(solution)/shard_map/jvp()/gather | solution.py:23
  255.3 10.0 %broadcast_select_fusion = f32[128,128,128]{2,1,0:T(8,128)} fusion(f32[128,128,128]{2,1,0:T(8,128)} %bitcast.82, pred[128,128]{1,0:T(8,128)(4,1)} %subtract_compare_fusion), kind=kLoop, calls=%fused_computation.4 | loop fusion | flops 2097152 | bytes 16793600 | tf_op jit(solution)/shard_map/jvp(jit(_where))/select_n | solution.py:23
  265.3 9.3 %copy.126 = f32[128,128,128]{1,0,2:T(8,128)} copy(f32[128,128,128]{2,1,0:T(8,128)} %broadcast_select_fusion) | data formatting | bytes 16777216 | tf_op jit(solution)/shard_map/jvp(jit(_where))/select_n | solution.py:23
  274.6 10.1 %fusion.9 = bf16[8,128,128]{1,0,2:T(8,128)(2,1)S(1)} fusion(f32[128,8,128]{2,1,0:T(8,128)} %fusion.13, f32[128,128,128]{1,0,2:T(8,128)} %copy.126, bf16[128,8,128]{0,2,1:T(8,128)(2,1)} %all-to-all-done), kind=kOutput, calls=%fused_computation.26 | convolution fusion | flops 201588736 | bytes 9437184 | tf_op jit(solution)/shard_map/jvp(ijc,bjc->bic)/dot_general | solution.py:41
  284.7 12.0 %all_to_all.43 = bf16[8,128,128]{1,2,0:T(8,128)(2,1)S(1)} all-to-all(bf16[8,128,128]{1,2,0:T(8,128)(2,1)S(1)} %copy.130), channel_id=1, replica_groups=mesh['ctx'=8,'tp'=4] {'ctx'}, dimensions={0} | all-to-all | bytes 524288 | tf_op jit(solution)/shard_map/all_to_all | solution.py:55
  297.5 2.0 copy.152
  299.6 17.4 %convolution_bitcast_fusion = f32[8192,1024]{0,1:T(8,128)} fusion(bf16[128,8192]{1,0:T(8,128)(2,1)} %all-gather.2.cloned.1.call-done, f32[128,1024]{1,0:T(8,128)} %copy.152, f32[128,3,1024]{2,0,1:T(8,128)S(1)} %multiply_add_fusion), kind=kOutput, calls=%fused_computation.2 | convolution fusion | flops 2147745792 | bytes 36700160 | tf_op jit(solution)/shard_map/dot_general | solution.py:81
  317.0 1.3 split.21
  320.4 1.4 multiply_add_fusion.1
  321.9 2.6 pad.113
  325.4 1.0 copy.135
  326.4 2.2 fusion.15
  328.6 7.5 fusion.8
  336.2 19.2 %all_to_all.44 = bf16[8,128,128]{1,2,0:T(8,128)(2,1)S(1)} all-to-all(bf16[8,128,128]{1,2,0:T(8,128)(2,1)S(1)} %copy.137), channel_id=1, replica_groups=mesh['ctx'=8,'tp'=4] {'ctx'}, dimensions={0} | all-to-all | bytes 524288 | tf_op jit(solution)/shard_map/all_to_all | solution.py:55
  356.2 2.0 copy.154
  358.2 1.3 multiply_bitcast_fusion
  361.0 1.6 collective-permute-start.1
  362.6 3.2 fusion.5
  366.0 1.3 collective-permute-done.1
  367.4 1.4 pad_maximum_fusion
  368.8 1.9 multiply_reduce_fusion.2
  370.7 3.0 collective-permute-start.2
  379.2 5.8 collective-permute-done.3
  385.0 31.8 %all_gather.11 = f32[16,1024]{1,0:T(8,128)S(1)} all-gather(f32[16,128]{1,0:T(8,128)S(1)} %get-tuple-element.56), channel_id=1, replica_groups=mesh['ctx'=8,'tp'=4] {'ctx'}, dimensions={1}, use_global_device_ids=true | all-gather | bytes 73728 | tf_op jit(solution)/shard_map/all_gather | solution.py:98
  416.8 31.6 %all_gather.10 = f32[16,1024]{1,0:T(8,128)S(1)} all-gather(f32[16,128]{1,0:T(8,128)S(1)} %get-tuple-element.57), channel_id=1, replica_groups=mesh['ctx'=8,'tp'=4] {'ctx'}, dimensions={1}, use_global_device_ids=true | all-gather | bytes 73728 | tf_op jit(solution)/shard_map/all_gather | solution.py:97
  449.1 417.8 %reduce-scatter.2.cloned.1.call-done = f32[1024,1024]{0,1:T(8,128)} async-done(((f32[8192,1024]{0,1:T(8,128)}), f32[1024,1024]{0,1:T(8,128)}) %reduce-scatter.2.cloned.1.call-update) | async-done | bytes 4194320 | tf_op jit(solution)/shard_map/reduce_scatter | solution.py:80
  866.9 5.3 copy.150
  (142 shorter events, 29.2 us)
Async XLA Ops:
  7.2 31.6 %all-gather.2.cloned.1.call-start = ((), (), s32[]{:S(2)}) async-start(), calls=%async_computation.5 | async-start | bytes 2621440 | tf_op jit(solution)/shard_map/all_gather | solution.py:79
  8.7 7.7 collective-permute-start
  13.6 21.0 %copy-start.28 = (f32[128]{0:T(128)}, f32[128]{0:T(128)S(1)}, u32[]{:S(2)}) copy-start(f32[128]{0:T(128)S(1)} %broadcast_subtract_fusion) | copy-start | bytes 1540
  15.0 23.7 %copy-start.23 = (f32[16,128]{1,0:T(8,128)}, f32[16,128]{1,0:T(8,128)S(1)}, u32[]{:S(2)}) copy-start(f32[16,128]{1,0:T(8,128)S(1)} %get-tuple-element.51) | copy-start | bytes 24580
  15.8 2.5 copy-start.10
  15.8 2.5 copy-start.12
  15.8 2.5 copy-start.14
  20.8 13.8 %all-to-all-start = ((bf16[128,8,128]{0,2,1:T(8,128)(2,1)}), bf16[128,8,128]{0,2,1:T(8,128)(2,1)}, u32[]{:S(2)}, u32[]{:S(2)}) async-start(bf16[128,8,128]{0,2,1:T(8,128)(2,1)} %bitcast.87), calls=%async_computation | async-start | bytes 524288 | tf_op jit(solution)/shard_map/all_to_all | solution.py:51
  38.7 19.2 %copy-start.25 = (f32[2,16,128]{2,1,0:T(8,128)}, f32[2,16,128]{2,1,0:T(8,128)S(1)}, u32[]{:S(2)}) copy-start(f32[2,16,128]{2,1,0:T(8,128)S(1)} %slice_add_fusion.3) | copy-start | bytes 49156
  53.5 12.3 %all-to-all-start.2 = ((bf16[128,8,128]{0,2,1:T(8,128)(2,1)}), bf16[128,8,128]{0,2,1:T(8,128)(2,1)}, u32[]{:S(2)}, u32[]{:S(2)}) async-start(bf16[128,8,128]{0,2,1:T(8,128)(2,1)} %bitcast.86), calls=%async_computation.2 | async-start | bytes 524288 | tf_op jit(solution)/shard_map/all_to_all | solution.py:51
  57.5 809.4 %reduce-scatter.2.cloned.1.call-start = ((), (), s32[]{:S(2)}) async-start(), calls=%async_computation.6 | async-start | bytes 37748736 | tf_op jit(solution)/shard_map/reduce_scatter | solution.py:80
  57.9 0.6 copy-start.19
  57.9 0.6 copy-start.21
  71.5 2.0 copy-start.18
  77.1 3.3 copy-start.9
  317.0 1.4 copy-start.8
  317.0 1.4 copy-start.20
  317.0 1.4 copy-start.22
  317.0 2.0 copy-start.26
  317.0 2.0 copy-start.24
  317.0 2.0 copy-start.30
  358.2 1.4 copy-start.6
  359.6 0.8 copy-start
  359.7 6.1 copy-start.2
  359.7 6.1 copy-start.4
  359.7 2.9 copy-start.7
  359.7 2.9 copy-start.29
  360.4 5.5 copy-start.27
  360.4 5.5 copy-start.17
  360.4 5.6 copy-start.16
  361.0 6.4 copy-start.1
  361.0 6.4 collective-permute-start.1
  365.9 2.8 copy-start.3
  365.9 2.8 copy-start.5
  366.0 2.8 copy-start.11
  366.0 2.8 copy-start.13
  366.0 2.8 copy-start.15
  370.7 7.6 collective-permute-start.2
  378.3 6.6 collective-permute-start.3
  384.9 63.5 %collective-permute-start.4 = (f32[3,3,1024]{2,1,0:T(4,128)S(1)}, f32[3,3,1024]{2,1,0:T(4,128)S(1)}, u32[]{:S(2)}, u32[]{:S(2)}) collective-permute-start(f32[3,3,1024]{2,1,0:T(4,128)S(1)} %fusion.68), channel_id=1, source_target_pairs={{0,16},{4,20},{8,24},{12,28},{16,0},{20,4},{24,8},{28,12},{1,17},{... | collective-permute-start | bytes 110600 | tf_op jit(solution)/shard_map/ppermute | solution.py:121
Sparse Core Ops, SparseCore 0:
  9.6 25.2 all-gather.1
  317.2 549.7 reduce-scatter.1
